TPU v7x, 32 devices: a whole 2x2x4 slice. The times are simulated.
32 devices in a mesh: ens: 2 (over y), lon: 16 (over z, x, core).
Axes of the slice: x: 2, y: 2, z: 4, core: 2. Of those that a mesh axis runs over, the one named last changes fastest.
Arguments:
- saved_input: bfloat16 [32, 192, 16, 128], P(('ens', 'lon')), parts along dimension 0, may hold values from -127 to 127, as said below
- tile_scale: float32 [32, 8, 192], P(('ens', 'lon')), parts along dimension 0, may hold values from 0.002 to 0.03
- ocean_tiles: int32 [32, 8], P(('ens', 'lon')), parts along dimension 0, may hold values from 0 to 1, as said below
- upstream: bfloat16 [32, 192, 16, 128], P(('ens', 'lon')), parts along dimension 0, may hold values from -6 to 6
- kernel: float32 [49, 192], replicated, may hold values from -0.875 to 0.875
- kernel_offset: float32 [192], replicated, may hold values from -3 to 3
- norm_gain: float32 [192], replicated, may hold values from 0.5 to 2
- norm_shift: float32 [192], replicated, may hold values from -3 to 3
- lift_weight: bfloat16 [192, 768], replicated, may hold values from -0.4375 to 0.4375
- lift_bias: float32 [768], replicated, may hold values from -3 to 3
- drop_weight: bfloat16 [768, 192], replicated, may hold values from -0.21875 to 0.21875
Outputs:
- grad_input: bfloat16 [32, 192, 16, 128], P(('ens', 'lon')), parts along dimension 0
- grad_kernel: float32 [98, 192], P('ens'), parts along dimension 0
- grad_offset: float32 [384], P('ens'), parts along dimension 0
- grad_gain: float32 [384], P('ens'), parts along dimension 0
- grad_shift: float32 [384], P('ens'), parts along dimension 0
- grad_lift: float32 [384, 768], P('ens'), parts along dimension 0
- grad_bias: float32 [1536], P('ens'), parts along dimension 0
- grad_drop: float32 [1536, 192], P('ens'), parts along dimension 0
There are 2 independent parts, one for each index of `ens`. A program takes and returns all parts, laid end to end along the dimension named above; an argument that names none is the same for every part. Nothing has to cross between parts.
Inputs may be any that keep to these rules, and one draw needn't show every extreme that they name: `saved_input`: whole numbers. `ocean_tiles`: some block holds no ocean tile.
All inputs are finite; a program needn't handle non-finite values.
Results may differ from a plain program's by a relative error of at most 0.0068.
Values may be sent and summed in bfloat16 or wider, within the bound.
A program may use at most 64 MiB of HBM per device.

v0:
```python
import math

import jax
import jax.numpy as jnp
from jax import lax
from jax.sharding import PartitionSpec as P

LAT_DEVS = 8


EPSILON = 1e-06


def with_halo(cells, sides, width):
    for axis, dim in sides:
        count = lax.axis_size(axis)
        head = lax.slice_in_dim(cells, 0, width, axis=dim)
        tail = lax.slice_in_dim(cells, cells.shape[dim] - width, cells.shape[dim], axis=dim)
        cells = jnp.concatenate(
            [
                lax.ppermute(tail, axis, [(i, (i + 1) % count) for i in range(count)]),
                cells,
                lax.ppermute(head, axis, [((i + 1) % count, i) for i in range(count)]),
            ],
            axis=dim,
        )
    return cells


def passed_along(x, axis, by):
    peers = lax.axis_size(axis)
    return lax.ppermute(x, axis, [(i, (i + by) % peers) for i in range(peers)])


def gelu_tanh(value):
    return jax.nn.gelu(value, approximate=True)


def depthwise(padded, kernel, offset, tile_rows, block_cols, span):
    total = jnp.zeros((padded.shape[0], tile_rows, block_cols), jnp.float32) + offset[:, None, None]
    for tap_row in range(span):
        for tap_col in range(span):
            weight = kernel[tap_row * span + tap_col][:, None, None]
            total = total + weight * padded[
                :, tap_row : tap_row + tile_rows, tap_col : tap_col + block_cols
            ].astype(jnp.float32)
    return total


def mlp_backward(pre_norm, cotangent, norm_gain, norm_shift, lift_weight, lift_bias, drop_weight):
    centre = pre_norm - jnp.mean(pre_norm, axis=0, keepdims=True)
    inverse = lax.rsqrt(jnp.mean(centre * centre, axis=0, keepdims=True) + EPSILON)
    normed = centre * inverse
    lifted = (normed * norm_gain[:, None] + norm_shift[:, None]).astype(jnp.bfloat16)
    hidden = jnp.dot(lift_weight.T, lifted, preferred_element_type=jnp.float32) + lift_bias[:, None]
    activated, gelu_back = jax.vjp(gelu_tanh, hidden)
    activated = activated.astype(jnp.bfloat16)
    drop_grad = jnp.dot(activated, cotangent.T, preferred_element_type=jnp.float32)
    act_grad = jnp.dot(drop_weight, cotangent, preferred_element_type=jnp.float32)
    hidden_grad = gelu_back(act_grad)[0]
    bias_grad = jnp.sum(hidden_grad, axis=1)
    hidden_round = hidden_grad.astype(jnp.bfloat16)
    lift_grad = jnp.dot(lifted, hidden_round.T, preferred_element_type=jnp.float32)
    lifted_grad = jnp.dot(lift_weight, hidden_round, preferred_element_type=jnp.float32)
    gain_grad = jnp.sum(lifted_grad * normed, axis=1)
    shift_grad = jnp.sum(lifted_grad, axis=1)
    normed_grad = lifted_grad * norm_gain[:, None]
    pre_grad = inverse * (
        normed_grad
        - jnp.mean(normed_grad, axis=0, keepdims=True)
        - normed * jnp.mean(normed_grad * normed, axis=0, keepdims=True)
    )
    return (pre_grad.astype(jnp.bfloat16), (lift_grad, drop_grad, bias_grad, gain_grad, shift_grad))


def conv_backward(padded_x, padded_d, kernel, tile_rows, block_cols, span):
    reach = span // 2
    pre_grad = padded_d[:, reach : reach + tile_rows, reach : reach + block_cols].astype(
        jnp.float32
    )
    kernel_terms = []
    input_grad = jnp.zeros((padded_x.shape[0], tile_rows, block_cols), jnp.float32)
    for tap_row in range(span):
        for tap_col in range(span):
            window = padded_x[
                :, tap_row : tap_row + tile_rows, tap_col : tap_col + block_cols
            ].astype(jnp.float32)
            kernel_terms.append(jnp.sum(pre_grad * window, axis=(1, 2)))
            flipped = padded_d[
                :,
                2 * reach - tap_row : 2 * reach - tap_row + tile_rows,
                2 * reach - tap_col : 2 * reach - tap_col + block_cols,
            ].astype(jnp.float32)
            input_grad = input_grad + kernel[tap_row * span + tap_col][:, None, None] * flipped
    return (jnp.stack(kernel_terms), jnp.sum(pre_grad, axis=(1, 2)), input_grad)


def extend(field, reach):
    tile_rows = field.shape[1]
    block_cols = field.shape[2]
    widened = with_halo(field, (("lon", 1),), reach)
    row_place = (lax.axis_index("lon") + 1) % LAT_DEVS
    keep_lower = (row_place != 0).astype(field.dtype)
    keep_upper = (row_place != LAT_DEVS - 1).astype(field.dtype)
    lower = widened[:, :reach] * keep_lower
    upper = widened[:, reach + tile_rows :] * keep_upper
    rows_done = jnp.concatenate([lower, field, upper], axis=1)
    western = passed_along(rows_done[:, :, block_cols - reach :], "lon", LAT_DEVS)
    eastern = passed_along(rows_done[:, :, :reach], "lon", -LAT_DEVS)
    return jnp.concatenate([western, rows_done, eastern], axis=2)


def body(
    saved_input,
    tile_scale,
    ocean_tiles,
    upstream,
    kernel,
    kernel_offset,
    norm_gain,
    norm_shift,
    lift_weight,
    lift_bias,
    drop_weight,
):
    channels = saved_input.shape[1]
    tile_rows = saved_input.shape[2]
    block_cols = saved_input.shape[3]
    slot_count = block_cols // tile_rows
    hidden_width = lift_weight.shape[1]
    span = math.isqrt(kernel.shape[0])
    reach = span // 2
    ocean = ocean_tiles[0]
    mask_cells = jnp.repeat(ocean, tile_rows).astype(jnp.float32)
    scale_cells = jnp.repeat(tile_scale[0].T, tile_rows, axis=1)
    field = (saved_input[0].astype(jnp.float32) * scale_cells[:, None, :] * mask_cells).astype(
        jnp.bfloat16
    )
    cotangent = upstream[0] * mask_cells.astype(jnp.bfloat16)
    padded_x = extend(field, reach)
    pre_norm = depthwise(padded_x, kernel, kernel_offset, tile_rows, block_cols, span)
    zero_grads = (
        jnp.zeros((channels, hidden_width), jnp.float32),
        jnp.zeros((hidden_width, channels), jnp.float32),
        jnp.zeros((hidden_width,), jnp.float32),
        jnp.zeros((channels,), jnp.float32),
        jnp.zeros((channels,), jnp.float32),
    )
    tile_cells = tile_rows * tile_rows

    def compute(operands):
        return mlp_backward(
            operands[0], operands[1], norm_gain, norm_shift, lift_weight, lift_bias, drop_weight
        )

    def to_tiles(block):
        shaped = block.reshape(channels, tile_rows, slot_count, tile_rows)
        return jnp.transpose(shaped, (2, 0, 1, 3)).reshape(slot_count, channels, tile_cells)

    pre_tiles = to_tiles(pre_norm)
    cot_tiles = to_tiles(cotangent)

    def tile_step(carry, operands):
        piece, tile_cot, alive = operands
        tile_grad, grads = compute((piece, tile_cot))
        return (jax.tree.map(jnp.add, carry, grads), tile_grad)

    grads, tile_grads = lax.scan(tile_step, zero_grads, (pre_tiles, cot_tiles, ocean))
    lift_grad, drop_grad, bias_grad, gain_grad, shift_grad = grads
    grad_field = jnp.transpose(
        tile_grads.reshape(slot_count, channels, tile_rows, tile_rows), (1, 2, 0, 3)
    ).reshape(channels, tile_rows, block_cols)
    padded_d = extend(grad_field, reach)
    kernel_sum, offset_sum, conv_grad = conv_backward(
        padded_x, padded_d, kernel, tile_rows, block_cols, span
    )
    lift_grad, drop_grad, bias_grad, gain_grad, shift_grad, kernel_sum, offset_sum = lax.psum(
        (lift_grad, drop_grad, bias_grad, gain_grad, shift_grad, kernel_sum, offset_sum), "lon"
    )
    factor = 1.0 / math.sqrt(lax.axis_size("lon") * tile_rows * block_cols)
    grad_input = (mask_cells * (cotangent.astype(jnp.float32) + conv_grad)).astype(jnp.bfloat16)[
        None
    ]
    return (
        grad_input,
        kernel_sum * factor,
        offset_sum * factor,
        gain_grad * factor,
        shift_grad * factor,
        lift_grad * factor,
        bias_grad * factor,
        drop_grad * factor,
    )


def solution(mesh):
    return jax.shard_map(
        body,
        mesh=mesh,
        in_specs=(
            P(("ens", "lon"), None, None, None),
            P(("ens", "lon"), None, None),
            P(("ens", "lon"), None),
            P(("ens", "lon"), None, None, None),
            P(),
            P(),
            P(),
            P(),
            P(),
            P(),
            P(),
        ),
        out_specs=(
            P(("ens", "lon"), None, None, None),
            P("ens", None),
            P("ens"),
            P("ens"),
            P("ens"),
            P("ens", None),
            P("ens"),
            P("ens", None),
        ),
        check_vma=False,
    )
```

profile of v0, /device:TPU:0, one launch (start us, length us, event | category | flops | bytes accessed | tf_op | source)
XLA Modules:
  0.0 396.6 jit_solution(15375810616551937688)
XLA Ops:
  12.2 5.4 %collective-permute-start.1 = (bf16[192,3,128]{0,2,1:T(8,128)(2,1)S(1)}, bf16[192,3,128]{0,2,1:T(8,128)(2,1)S(1)}, u32[]{:S(2)}, u32[]{:S(2)}) collective-permute-start(bf16[192,3,128]{0,2,1:T(8,128)(2,1)S(1)} %get-tuple-element.374), channel_id=1, source_target_pairs={{1,0},{2,1},{3,2},{4,3},{5,4},{6,5},{7,6},{8,7},{9,8},{10,9},{11,1... | collective-permute-start | bytes 442376 | tf_op jit(solution)/shard_map/ppermute | solution.py:23
  21.0 4.8 %collective-permute-done = bf16[192,3,128]{0,2,1:T(8,128)(2,1)} collective-permute-done((bf16[192,3,128]{0,2,1:T(8,128)(2,1)}, bf16[192,3,128]{0,2,1:T(8,128)(2,1)}, u32[]{:S(2)}, u32[]{:S(2)}) %collective-permute-start) | collective-permute-done | bytes 147488 | tf_op jit(solution)/shard_map/ppermute | solution.py:21
  26.9 2.9 collective-permute-start.3
  37.7 22.1 %fusion.77 = f32[192,16,128]{0,2,1:T(8,128)S(1)} fusion(bf16[192,16,128]{0,2,1:T(8,128)(2,1)S(1)} %copy-done.4, bf16[192,3,128]{0,2,1:T(8,128)(2,1)S(1)} %broadcast_multiply_fusion.6, bf16[192,3,128]{0,2,1:T(8,128)(2,1)S(1)} %broadcast_multiply_fusion.8, f32[192]{0:T(256)} %bitcast.375, f32[192]{0:T(256)} %bitcast.377, f32[192]{0:T(256)S(1)} %bitcast.321, ...), kind=kLoop, calls=%fused_computation.198 | loop fusion | flops 60162048 | bytes 35722752 | tf_op jit(solution)/shard_map/add | solution.py:44
  61.5 2.8 copy.29
  64.3 143.0 %while.23 = (s32[]{:T(128)}, f32[192,768]{1,0:T(8,128)}, f32[768,192]{0,1:T(8,128)}, f32[768]{0:T(1024)}, f32[192]{0:T(256)}, /*index=5*/f32[192]{0:T(256)}, bf1...) while((s32[]{:T(128)}, f32[192,768]{1,0:T(8,128)}, ...), condition=%wide.region_8.9_spmd.clone, body=%wide.region_0.8_spmd.clone.sunk | while | flops 385697152 | bytes 13668770 | solution.py:168
  67.6 2.6 fusion.194
  85.1 2.6 fusion.194
  94.1 2.4 convolution_add_fusion.5
  96.5 2.6 convolution_add_fusion.6
  103.0 2.6 fusion.194
  112.0 2.4 convolution_add_fusion.5
  114.4 2.6 convolution_add_fusion.6
  121.0 2.6 fusion.194
  132.4 2.6 convolution_add_fusion.6
  138.9 2.6 fusion.194
  150.3 2.6 convolution_add_fusion.6
  156.8 2.6 fusion.194
  168.2 2.6 convolution_add_fusion.6
  174.7 2.6 fusion.194
  186.1 2.6 convolution_add_fusion.6
  192.7 2.6 fusion.194
  204.1 2.6 convolution_add_fusion.6
  210.9 6.9 %fusion.151 = (f32[192]{0:T(256)S(1)}, f32[192]{0:T(256)S(1)}, f32[192]{0:T(256)S(1)}, f32[192]{0:T(256)S(1)}, f32[192]{0:T(256)S(1)}, /*index=5*/f32[192]{0:T(2...) fusion(bf16[192,22,131]{0,2,1:T(8,128)(2,1)S(1)} %get-tuple-ele, ...), kind=kLoop, calls=%fused_computation.272 | loop fusion | flops 21623424 | bytes 14956032 | tf_op jit(solution)/shard_map/reduce_sum | solution.py:88
  217.8 6.5 %fusion.147 = (f32[192]{0:T(256)S(1)}, f32[192]{0:T(256)S(1)}, f32[192]{0:T(256)S(1)}, f32[192]{0:T(256)S(1)}, f32[192]{0:T(256)S(1)}, /*index=5*/f32[192]{0:T(2...) fusion(bf16[192,22,131]{0,2,1:T(8,128)(2,1)S(1)} %get-tuple-ele, ...), kind=kLoop, calls=%fused_computation.268 | loop fusion | flops 21623424 | bytes 14956032 | tf_op jit(solution)/shard_map/reduce_sum | solution.py:88
  224.4 4.8 %fusion.148 = (f32[192]{0:T(256)S(1)}, f32[192]{0:T(256)S(1)}, f32[192]{0:T(256)S(1)}, f32[192]{0:T(256)S(1)}, f32[192]{0:T(256)S(1)}, /*index=5*/f32[192]{0:T(2...) fusion(bf16[192,3,128]{0,2,1:T(8,128)(2,1)S(1)} %copy-done.14, ...), kind=kLoop, calls=%fused_computation.269 | loop fusion | flops 16905984 | bytes 6595584 | tf_op jit(solution)/shard_map/reduce_sum | solution.py:88
  230.3 57.7 %all-reduce = (f32[49,192]{1,0:T(8,128)S(1)}, f32[192]{0:T(256)S(1)}, f32[192]{0:T(256)S(1)}, f32[192]{0:T(256)S(1)}, f32[768]{0:T(1024)S(1)}) all-reduce(f32[49,192]{1,0:T(8,128)S(1)} %stack.199, f32[192]{0:T(256)S(1)} %get-tuple-element.313, f32[192]{0:T(256)S(1)} %copy-done.27, ...), channel_id=1, replica_groups=mesh['ens'=2,'lon'=16] {'lon'}, use_global_device_ids=true, to_apply=%region_58.59 | all-reduce | flops 10752 | bytes 86016 | tf_op jit(solution)/shard_map/psum | solution.py:177
  289.4 4.4 %collective-permute-start.5 = (bf16[192,3,128]{0,2,1:T(8,128)(2,1)S(1)}, bf16[192,3,128]{0,2,1:T(8,128)(2,1)S(1)}, u32[]{:S(2)}, u32[]{:S(2)}) collective-permute-start(bf16[192,3,128]{0,2,1:T(8,128)(2,1)S(1)} %get-tuple-element.372), channel_id=1, source_target_pairs={{1,0},{2,1},{3,2},{4,3},{5,4},{6,5},{7,6},{8,7},{9,8},{10,9},{11,1... | collective-permute-start | bytes 442376 | tf_op jit(solution)/shard_map/ppermute | solution.py:23
  294.4 3.1 collective-permute-done.4
  298.4 2.9 collective-permute-start.7
  305.8 18.3 %fusion.164 = bf16[1,192,16,128]{1,3,2,0:T(8,128)(2,1)S(1)} fusion(bf16[192,22,131]{0,2,1:T(8,128)(2,1)S(1)} %get-tuple-element.364, f32[192]{0:T(256)} %bitcast.376, f32[192]{0:T(256)} %bitcast.378, f32[192]{0:T(256)S(1)} %bitcast.322, bf16[192,16,128]{0,2,1:T(8,128)(2,1)S(1)} %bitcast.270, bf16[192,3,128]{0,2,1:T(8,128)(2,1)S(1)} %broadcast_multiply_fusion.7, ...), kind=kLoop, calls=%fused_computation.314 | loop fusion | flops 61734912 | bytes 35722752 | tf_op jit(solution)/shard_map/broadcast_in_dim | solution.py:181
  325.5 60.4 %all-reduce.4.cloned.1.call-done = (f32[192,768]{1,0:T(8,128)}, f32[768,192]{0,1:T(8,128)}) async-done(((f32[192,768]{1,0:T(8,128)}, f32[768,192]{0,1:T(8,128)}), (f32[192,768]{1,0:T(8,128)}, f32[768,192]{0,1:T(8,128)})) %all-reduce.4.cloned.1.call-update) | async-done | bytes 1179664 | tf_op jit(solution)/shard_map/psum | solution.py:177
  (489 shorter events, 133.1 us)
Async XLA Ops:
  7.2 378.7 %all-reduce.4.cloned.1.call-start = ((), (), s32[]{:S(2)}) async-start(), calls=%async_computation | async-start | bytes 2359296 | tf_op jit(solution)/shard_map/psum | solution.py:177
  8.6 9.0 %copy-start.26 = (f32[49,192]{1,0:T(8,128)S(1)}, f32[49,192]{1,0:T(8,128)}, u32[]{:S(2)}) copy-start(f32[49,192]{1,0:T(8,128)} %param.17) | copy-start | bytes 112900
  8.6 9.7 %copy-start.18 = (bf16[1,192,16,128]{3,2,1,0:T(8,128)(2,1)S(1)}, bf16[1,192,16,128]{3,2,1,0:T(8,128)(2,1)}, u32[]{:S(2)}) copy-start(bf16[1,192,16,128]{3,2,1,0:T(8,128)(2,1)} %param.16) | copy-start | bytes 2359300
  10.2 7.4 %copy-start.10 = (bf16[1,192,16,128]{1,3,2,0:T(8,128)(2,1)}, bf16[1,192,16,128]{1,3,2,0:T(8,128)(2,1)S(1)}, u32[]{:S(2)}) copy-start(bf16[1,192,16,128]{1,3,2,0:T(8,128)(2,1)S(1)} %copy.25) | copy-start | bytes 2359300
  11.4 15.3 %copy-start.3 = (bf16[192,16,128]{0,2,1:T(8,128)(2,1)}, bf16[192,16,128]{0,2,1:T(8,128)(2,1)S(1)}, u32[]{:S(2)}) copy-start(bf16[192,16,128]{0,2,1:T(8,128)(2,1)S(1)} %fusion.153) | copy-start | bytes 2359300
  12.2 8.7 %collective-permute-start.1 = (bf16[192,3,128]{0,2,1:T(8,128)(2,1)S(1)}, bf16[192,3,128]{0,2,1:T(8,128)(2,1)S(1)}, u32[]{:S(2)}, u32[]{:S(2)}) collective-permute-start(bf16[192,3,128]{0,2,1:T(8,128)(2,1)S(1)} %get-tuple-element.374), channel_id=1, source_target_pairs={{1,0},{2,1},{3,2},{4,3},{5,4},{6,5},{7,6},{8,7},{9,8},{10,9},{11,1... | collective-permute-start | bytes 442376 | tf_op jit(solution)/shard_map/ppermute | solution.py:23
  17.6 8.2 %collective-permute-start = (bf16[192,3,128]{0,2,1:T(8,128)(2,1)}, bf16[192,3,128]{0,2,1:T(8,128)(2,1)}, u32[]{:S(2)}, u32[]{:S(2)}) collective-permute-start(bf16[192,3,128]{0,2,1:T(8,128)(2,1)} %get-tuple-element.373), channel_id=1, source_target_pairs={{0,1},{1,2},{2,3},{3,4},{4,5},{5,6},{6,7},{7,8},{8,9},{9,10},{10,1... | collective-permute-start | bytes 442376 | tf_op jit(solution)/shard_map/ppermute | solution.py:21
  18.3 19.0 %copy-start.30 = (f32[1,192]{1,0:T(1,128)}, f32[1,192]{1,0:T(1,128)S(1)}, u32[]{:S(2)}) copy-start(f32[1,192]{1,0:T(1,128)S(1)} %get-tuple-element.394) | copy-start | bytes 2308
  18.3 19.0 %copy-start.32 = (f32[1,192]{1,0:T(1,128)}, f32[1,192]{1,0:T(1,128)S(1)}, u32[]{:S(2)}) copy-start(f32[1,192]{1,0:T(1,128)S(1)} %get-tuple-element.395) | copy-start | bytes 2308
  19.0 7.8 %copy-start.8 = (bf16[1,192,16,128]{1,3,2,0:T(8,128)(2,1)}, bf16[1,192,16,128]{1,3,2,0:T(8,128)(2,1)S(1)}, u32[]{:S(2)}) copy-start(bf16[1,192,16,128]{1,3,2,0:T(8,128)(2,1)S(1)} %copy.24) | copy-start | bytes 2359300
  19.0 12.4 %copy-start.111 = (f32[128]{0:T(128)S(1)}, f32[128]{0:T(128)}, u32[]{:S(2)}) copy-start(f32[128]{0:T(128)} %copy-done.110) | copy-start | bytes 1540
  21.0 16.3 %copy-start.13 = (bf16[192,3,128]{0,2,1:T(8,128)(2,1)}, bf16[192,3,128]{0,2,1:T(8,128)(2,1)S(1)}, u32[]{:S(2)}) copy-start(bf16[192,3,128]{0,2,1:T(8,128)(2,1)S(1)} %broadcast_multiply_fusion.6) | copy-start | bytes 442372
  26.7 10.6 %copy-start.15 = (bf16[192,3,128]{0,2,1:T(8,128)(2,1)}, bf16[192,3,128]{0,2,1:T(8,128)(2,1)S(1)}, u32[]{:S(2)}) copy-start(bf16[192,3,128]{0,2,1:T(8,128)(2,1)S(1)} %broadcast_multiply_fusion.8) | copy-start | bytes 442372
  26.8 8.2 %collective-permute-start.2 = (bf16[192,22,3]{0,2,1:T(4,128)(2,1)S(1)}, bf16[192,22,3]{0,2,1:T(4,128)(2,1)S(1)}, u32[]{:S(2)}, u32[]{:S(2)}) collective-permute-start(bf16[192,22,3]{0,2,1:T(4,128)(2,1)S(1)} %get-tuple-element.369), channel_id=1, source_target_pairs={{0,8},{1,9},{2,10},{3,11},{4,12},{5,13},{6,14},{7,15},{8,0},{9,1},... | collective-permute-start | bytes 76040 | tf_op jit(solution)/shard_map/ppermute | solution.py:32
  26.9 8.1 %collective-permute-start.3 = (bf16[192,22,3]{0,2,1:T(4,128)(2,1)S(1)}, bf16[192,22,3]{0,2,1:T(4,128)(2,1)S(1)}, u32[]{:S(2)}, u32[]{:S(2)}) collective-permute-start(bf16[192,22,3]{0,2,1:T(4,128)(2,1)S(1)} %get-tuple-element.370), channel_id=1, source_target_pairs={{0,8},{1,9},{2,10},{3,11},{4,12},{5,13},{6,14},{7,15},{8,0},{9,1},... | collective-permute-start | bytes 76040 | tf_op jit(solution)/shard_map/ppermute | solution.py:32
  65.2 7.6 %copy-start.17 = (f32[256]{0:T(256)}, f32[256]{0:T(256)S(1)}, u32[]{:S(2)}) copy-start(f32[256]{0:T(256)S(1)} %broadcast_multiply_fusion.16) | copy-start | bytes 3076 | tf_op jit(solution)/shard_map/while
  82.8 7.6 %copy-start.17 = (f32[256]{0:T(256)}, f32[256]{0:T(256)S(1)}, u32[]{:S(2)}) copy-start(f32[256]{0:T(256)S(1)} %broadcast_multiply_fusion.16) | copy-start | bytes 3076 | tf_op jit(solution)/shard_map/while
  100.7 7.7 %copy-start.17 = (f32[256]{0:T(256)}, f32[256]{0:T(256)S(1)}, u32[]{:S(2)}) copy-start(f32[256]{0:T(256)S(1)} %broadcast_multiply_fusion.16) | copy-start | bytes 3076 | tf_op jit(solution)/shard_map/while
  110.7 6.9 %copy-start.21 = (f32[192]{0:T(256)S(1)}, f32[192]{0:T(256)}, u32[]{:S(2)}) copy-start(f32[192]{0:T(256)} %get-tuple-element.613) | copy-start | bytes 2308 | tf_op jit(solution)/shard_map/while
  118.6 7.6 %copy-start.17 = (f32[256]{0:T(256)}, f32[256]{0:T(256)S(1)}, u32[]{:S(2)}) copy-start(f32[256]{0:T(256)S(1)} %broadcast_multiply_fusion.16) | copy-start | bytes 3076 | tf_op jit(solution)/shard_map/while
  136.5 7.7 %copy-start.17 = (f32[256]{0:T(256)}, f32[256]{0:T(256)S(1)}, u32[]{:S(2)}) copy-start(f32[256]{0:T(256)S(1)} %broadcast_multiply_fusion.16) | copy-start | bytes 3076 | tf_op jit(solution)/shard_map/while
  146.6 6.9 %copy-start.21 = (f32[192]{0:T(256)S(1)}, f32[192]{0:T(256)}, u32[]{:S(2)}) copy-start(f32[192]{0:T(256)} %get-tuple-element.613) | copy-start | bytes 2308 | tf_op jit(solution)/shard_map/while
  154.5 7.6 %copy-start.17 = (f32[256]{0:T(256)}, f32[256]{0:T(256)S(1)}, u32[]{:S(2)}) copy-start(f32[256]{0:T(256)S(1)} %broadcast_multiply_fusion.16) | copy-start | bytes 3076 | tf_op jit(solution)/shard_map/while
  172.4 7.7 %copy-start.17 = (f32[256]{0:T(256)}, f32[256]{0:T(256)S(1)}, u32[]{:S(2)}) copy-start(f32[256]{0:T(256)S(1)} %broadcast_multiply_fusion.16) | copy-start | bytes 3076 | tf_op jit(solution)/shard_map/while
  182.4 6.9 %copy-start.21 = (f32[192]{0:T(256)S(1)}, f32[192]{0:T(256)}, u32[]{:S(2)}) copy-start(f32[192]{0:T(256)} %get-tuple-element.613) | copy-start | bytes 2308 | tf_op jit(solution)/shard_map/while
  190.3 7.6 %copy-start.17 = (f32[256]{0:T(256)}, f32[256]{0:T(256)S(1)}, u32[]{:S(2)}) copy-start(f32[256]{0:T(256)S(1)} %broadcast_multiply_fusion.16) | copy-start | bytes 3076 | tf_op jit(solution)/shard_map/while
  210.9 13.5 %copy-start = (bf16[192,16,8,16]{0,3,2,1:T(8,128)(2,1)}, bf16[192,16,8,16]{0,3,2,1:T(8,128)(2,1)S(1)}, u32[]{:S(2)}) copy-start(bf16[192,16,8,16]{0,3,2,1:T(8,128)(2,1)S(1)} %copy.32) | copy-start | bytes 2359300
  229.3 60.0 %copy-start.1 = (bf16[192,16,8,16]{0,3,2,1:T(8,128)(2,1)S(1)}, bf16[192,16,8,16]{0,3,2,1:T(8,128)(2,1)}, u32[]{:S(2)}) copy-start(bf16[192,16,8,16]{0,3,2,1:T(8,128)(2,1)} %copy-done) | copy-start | bytes 2359300
  289.3 8.2 %collective-permute-start.4 = (bf16[192,3,128]{0,2,1:T(8,128)(2,1)S(1)}, bf16[192,3,128]{0,2,1:T(8,128)(2,1)S(1)}, u32[]{:S(2)}, u32[]{:S(2)}) collective-permute-start(bf16[192,3,128]{0,2,1:T(8,128)(2,1)S(1)} %get-tuple-element.371), channel_id=1, source_target_pairs={{0,1},{1,2},{2,3},{3,4},{4,5},{5,6},{6,7},{7,8},{8,9},{9,10},{10,1... | collective-permute-start | bytes 442376 | tf_op jit(solution)/shard_map/ppermute | solution.py:21
  289.4 8.8 %collective-permute-start.5 = (bf16[192,3,128]{0,2,1:T(8,128)(2,1)S(1)}, bf16[192,3,128]{0,2,1:T(8,128)(2,1)S(1)}, u32[]{:S(2)}, u32[]{:S(2)}) collective-permute-start(bf16[192,3,128]{0,2,1:T(8,128)(2,1)S(1)} %get-tuple-element.372), channel_id=1, source_target_pairs={{1,0},{2,1},{3,2},{4,3},{5,4},{6,5},{7,6},{8,7},{9,8},{10,9},{11,1... | collective-permute-start | bytes 442376 | tf_op jit(solution)/shard_map/ppermute | solution.py:23
  298.3 5.3 %collective-permute-start.6 = (bf16[192,22,3]{0,2,1:T(4,128)(2,1)S(1)}, bf16[192,22,3]{0,2,1:T(4,128)(2,1)S(1)}, u32[]{:S(2)}, u32[]{:S(2)}) collective-permute-start(bf16[192,22,3]{0,2,1:T(4,128)(2,1)S(1)} %get-tuple-element.365), channel_id=1, source_target_pairs={{0,8},{1,9},{2,10},{3,11},{4,12},{5,13},{6,14},{7,15},{8,0},{9,1},... | collective-permute-start | bytes 76040 | tf_op jit(solution)/shard_map/ppermute | solution.py:32
  298.4 6.1 %collective-permute-start.7 = (bf16[192,22,3]{0,2,1:T(4,128)(2,1)S(1)}, bf16[192,22,3]{0,2,1:T(4,128)(2,1)S(1)}, u32[]{:S(2)}, u32[]{:S(2)}) collective-permute-start(bf16[192,22,3]{0,2,1:T(4,128)(2,1)S(1)} %get-tuple-element.366), channel_id=1, source_target_pairs={{0,8},{1,9},{2,10},{3,11},{4,12},{5,13},{6,14},{7,15},{8,0},{9,1},... | collective-permute-start | bytes 76040 | tf_op jit(solution)/shard_map/ppermute | solution.py:32
  (147 other events, 524.4 us)
Sparse Core Ops, SparseCore 0:
  294.0 91.8 all-reduce.3
where the time goes:
time: 399 us; the launch traced here: 397 us
  other arithmetic  118 us (30%)
  matrix products  86.8 us (22%)
  waiting for transfers between devices  71.3 us (18%)
  blocking collectives  57.7 us (14%)
  local copies, waits for them, and re-layouts  30.7 us (8%)
  starting transfers between devices  15.9 us (4%)
  between operations  15.8 us (4%)
    psum x1, waiting for transfers between devices, body(): lax.psum((lift_grad, drop_grad, bias_grad, gain_grad, shift_grad, kernel_...  60.4 us
    psum x1, blocking collectives, body(): lax.psum((lift_grad, drop_grad, bias_grad, gain_grad, shift_grad, kernel_...  57.7 us
    add x1, other arithmetic, depthwise(): total + weight * padded[:, tap_row:tap_row + tile_rows, tap_col:tap_col +...  22.1 us
    dot_general x8, matrix products, mlp_backward(): jnp.dot(drop_weight, cotangent, preferred_element_type=jnp.float32)  21 us
    dot_general x8, matrix products, mlp_backward(): jnp.dot(activated, cotangent.T, preferred_element_type=jnp.float32)  20.6 us
    dot_general x8, matrix products, mlp_backward(): jnp.dot(lifted, hidden_round.T, preferred_element_type=jnp.float32)  19.3 us
    reduce_sum x3, other arithmetic, conv_backward(): kernel_terms.append(jnp.sum(pre_grad * window, axis=(1, 2)))  18.3 us
    broadcast_in_dim x1, other arithmetic, body(): (mask_cells * (cotangent.astype(jnp.float32) + conv_grad)).astype(jnp.bfl...  18.3 us
  transfers between devices with their start and end apart: 9, of which 6 were waited for; matrix products, arithmetic and copies ran while one was open for 8% of the time, Pallas kernels for 0%

commit v1 on v0

v1 whole, which is shorter than its diff:
```python
import functools
import math

import jax
import jax.numpy as jnp
from jax import lax
from jax.experimental import pallas as pl
from jax.experimental.pallas import tpu as pltpu
from jax.sharding import PartitionSpec as P

LAT_DEVS = 8
EPSILON = 1e-06
MESH = pl.DeviceIdType.MESH
F32 = jnp.float32
BF16 = jnp.bfloat16


def lanes(shape):
    return lax.broadcasted_iota(jnp.int32, shape, len(shape) - 1)


def roll(x, shift):
    shift = shift % x.shape[-1]
    return x if shift == 0 else pltpu.roll(x, shift, x.ndim - 1)


class Dims:
    def __init__(self, n, channels, rows, cols, span, hidden):
        self.n, self.c, self.rows, self.cols, self.hidden = n, channels, rows, cols, hidden
        self.span, self.reach = span, span // 2
        self.ext = rows + 2 * self.reach
        self.same = 2 * LAT_DEVS == n


def neighbours(d):
    me = lax.axis_index("lon")
    north = lax.rem(me + d.n - 1, d.n)
    south = lax.rem(me + 1, d.n)
    east = lax.rem(me + LAT_DEVS, d.n)
    west = lax.rem(me + d.n - LAT_DEVS, d.n)
    return me, north, south, east, west


def pack_sides(d, main):
    k, r3 = d.reach, d.rows * d.reach

    def step(g, _):
        at = pl.ds(pl.multiple_of(g * 16, 16), 16)
        lane = lanes((16, d.cols))
        packed = jnp.zeros((16, d.cols), F32)
        for r in range(d.rows):
            x = main[r + k, at, :]
            lo, hi = r * k, r3 + r * k
            packed = jnp.where((lane >= lo) & (lane < lo + k), roll(x, lo), packed)
            packed = jnp.where((lane >= hi) & (lane < hi + k), roll(x, hi - (d.cols - k)), packed)
        return at, packed

    return step


def exchange(d, main, side, rows_out, rows_in, pack_out, pack_in, fwd_in, ssem, rsem):
    k = d.reach
    me, north, south, east, west = neighbours(d)

    def copy(src, dst, slot, peer):
        return pltpu.make_async_remote_copy(
            src_ref=src,
            dst_ref=dst,
            send_sem=ssem.at[slot],
            recv_sem=rsem.at[slot],
            device_id={"lon": peer},
            device_id_type=MESH,
        )

    for r in range(k):
        rows_out[0, r] = main[k + r].astype(BF16)
        rows_out[1, r] = main[d.rows + r].astype(BF16)
    to_north = copy(rows_out.at[0], rows_in.at[1], 0, north)
    to_south = copy(rows_out.at[1], rows_in.at[0], 1, south)
    to_north.start()
    to_south.start()
    build = pack_sides(d, main)

    def pack_step(g, carry):
        at, packed = build(g, None)
        pack_out[at, :] = packed.astype(BF16)
        return carry

    lax.fori_loop(0, d.c // 16, pack_step, 0)
    count = 1 if d.same else 2
    sides = [copy(pack_out, pack_in.at[0], 2, west)]
    if not d.same:
        sides.append(copy(pack_out, pack_in.at[1], 3, east))
    for one in sides:
        one.start()

    def finish():
        for one in sides:
            one.wait()
        forwards = []
        for j in range(count):
            forwards.append(copy(pack_in.at[j], fwd_in.at[0, j], 4 + j, south))
            forwards.append(copy(pack_in.at[j], fwd_in.at[1, j], 6 + j, north))
        for one in forwards:
            one.start()
        place = lax.rem(me + 1, LAT_DEVS)
        keep_lower = jnp.where(place != 0, 1.0, 0.0).astype(F32)
        keep_upper = jnp.where(place != LAT_DEVS - 1, 1.0, 0.0).astype(F32)
        r3 = d.rows * k
        last = count - 1

        def unpack(east_pack, west_pack, r):
            lane = lanes(east_pack.shape)
            right = roll(east_pack, -(r * k))
            left = roll(west_pack, (d.cols - k) - (r3 + r * k))
            return jnp.where(lane < d.cols // 2, right, left)

        def own_step(g, carry):
            at = pl.ds(pl.multiple_of(g * 16, 16), 16)
            e, w = pack_in[0, at, :].astype(F32), pack_in[last, at, :].astype(F32)
            for r in range(d.rows):
                side[k + r, at, :] = unpack(e, w, r)
            return carry

        lax.fori_loop(0, d.c // 16, own_step, 0)
        to_north.wait()
        to_south.wait()
        for r in range(k):
            main[r] = rows_in[0, r].astype(F32) * keep_lower
            main[k + d.rows + r] = rows_in[1, r].astype(F32) * keep_upper
        for one in forwards:
            one.wait()

        def corner_step(g, carry):
            at = pl.ds(pl.multiple_of(g * 16, 16), 16)
            ne, nw = fwd_in[0, 0, at, :].astype(F32), fwd_in[0, last, at, :].astype(F32)
            se, sw = fwd_in[1, 0, at, :].astype(F32), fwd_in[1, last, at, :].astype(F32)
            for r in range(k):
                side[r, at, :] = unpack(ne, nw, d.rows - k + r) * keep_lower
                side[k + d.rows + r, at, :] = unpack(se, sw, r) * keep_upper
            return carry

        lax.fori_loop(0, d.c // 16, corner_step, 0)

    return finish


def shifted(d, main, side, at, q):
    s = q - d.reach
    x = main[:, at, :]
    if s == 0:
        return x
    lane = lanes(x.shape)
    h = side[:, at, :]
    keep = lane < s if s > 0 else lane >= d.cols + s
    return roll(jnp.where(keep, h, x), -s)


def depthwise(d, main, side, taps, flip, start, store):
    def group(g, carry):
        at = pl.ds(pl.multiple_of(g * 8, 8), 8)
        weights = taps[at, :]
        acc = start(g, at)
        for q in range(d.span):
            xq = shifted(d, main, side, at, q)
            for p in range(d.span):
                t = p * d.span + q
                if flip:
                    t = d.span * d.span - 1 - t
                acc = acc + weights[:, t : t + 1][None] * xq[p : p + d.rows]
        store(g, at, acc)
        return carry

    lax.fori_loop(0, d.c // 8, group, 0)


def kernel_grads(d, main, side, dmain, small):
    def group(g, carry):
        at = pl.ds(pl.multiple_of(g * 8, 8), 8)
        grad = dmain[d.reach : d.reach + d.rows, at, :]
        lane = lanes((8, d.cols))
        out = small[at, :]
        total = jnp.sum(jnp.sum(grad, axis=0), axis=1, keepdims=True)
        out = jnp.where(lane == d.span * d.span, total, out)
        for q in range(d.span):
            xq = shifted(d, main, side, at, q)
            for p in range(d.span):
                term = jnp.sum(grad * xq[p : p + d.rows], axis=0)
                total = jnp.sum(term, axis=1, keepdims=True)
                out = jnp.where(lane == p * d.span + q, total, out)
        small[at, :] = out
        return carry

    lax.fori_loop(0, d.c // 8, group, 0)


def dot(a, b, dims=((1,), (0,))):
    return lax.dot_general(a, b, (dims, ((), ())), preferred_element_type=F32)


def mlp(d, pre, cot, gain, shift, lift_t, lift, bias, drop, dmain, big_lift, big_drop, gain_acc, shift_acc):
    step_rows = 4
    block = 256
    wide = step_rows * d.cols
    root = math.sqrt(2.0 / math.pi)
    big_lift[...] = jnp.zeros_like(big_lift)
    big_drop[...] = jnp.zeros_like(big_drop)
    gain_acc[...] = jnp.zeros_like(gain_acc)
    shift_acc[...] = jnp.zeros_like(shift_acc)

    def fold(x):
        return sum(x[:, j * d.cols : (j + 1) * d.cols] for j in range(step_rows))

    def step(i, carry):
        r0 = i * step_rows
        x = jnp.concatenate([pre[r0 + j] for j in range(step_rows)], axis=1)
        ct = jnp.concatenate([cot[r0 + j] for j in range(step_rows)], axis=1)
        centre = x - jnp.mean(x, axis=0, keepdims=True)
        inverse = lax.rsqrt(jnp.mean(centre * centre, axis=0, keepdims=True) + EPSILON)
        normed = centre * inverse
        lifted = (normed * gain[...] + shift[...]).astype(BF16)
        ones = jnp.where(
            lax.broadcasted_iota(jnp.int32, (64, wide), 0) == 0, 1.0, 0.0
        ).astype(BF16)
        lifted_one = jnp.concatenate([lifted, ones], axis=0)
        lifted_grad = jnp.zeros((d.c, wide), F32)
        for b in range(d.hidden // block):
            hs = slice(b * block, (b + 1) * block)
            v = dot(lift_t[hs, :], lifted) + bias[hs, :]
            act_grad = dot(drop[hs, :], ct)
            v2 = v * v
            half = 0.5 * jnp.tanh(v * (root + (root * 0.044715) * v2)) + 0.5
            act = v * half
            slope = half + (act * (1.0 - half)) * (2.0 * root + (6.0 * root * 0.044715) * v2)
            hidden_round = (act_grad * slope).astype(BF16)
            big_drop[hs, :] += dot(act.astype(BF16), ct, ((1,), (1,)))
            big_lift[hs, :] += dot(hidden_round, lifted_one, ((1,), (1,)))
            lifted_grad = lifted_grad + dot(lift[:, hs], hidden_round)
        gain_acc[...] += fold(lifted_grad * normed)
        shift_acc[...] += fold(lifted_grad)
        ng = lifted_grad * gain[...]
        m1 = jnp.mean(ng, axis=0, keepdims=True)
        m2 = jnp.mean(ng * normed, axis=0, keepdims=True)
        pg = (inverse * (ng - m1 - normed * m2)).astype(BF16).astype(F32)
        for j in range(step_rows):
            dmain[d.reach + r0 + j] = pg[:, j * d.cols : (j + 1) * d.cols]
        return carry

    lax.fori_loop(0, d.rows // step_rows, step, 0)


def kernel(
    d,
    saved, scale, mask, upstream, taps, offset, gain, shift, lift_t, lift, bias, drop,
    out, big_lift, big_drop, small,
    flat, main, side, dmain, dside, cot, pre, rows_out, rows_in, pack_out, pack_in, fwd_in,
    gain_acc, shift_acc, ssem, rsem,
):
    me, north, south, east, west = neighbours(d)
    peers = [north, south, west] if d.same else [north, south, west, east]
    barrier = pltpu.get_barrier_semaphore()
    for peer in peers:
        pl.semaphore_signal(barrier, inc=1, device_id={"lon": peer}, device_id_type=MESH)
    flat[...] = saved[0].astype(F32).reshape(d.c * d.rows, d.cols)
    for r in range(d.rows):
        row = flat[pl.ds(r, d.c, stride=d.rows), :]
        main[d.reach + r] = (row * scale[...]).astype(BF16).astype(F32)
    pl.semaphore_wait(barrier, len(peers))

    def ex(i, m, s):
        return exchange(
            d, m, s, rows_out.at[i], rows_in.at[i], pack_out.at[i], pack_in.at[i], fwd_in.at[i],
            ssem.at[i], rsem.at[i],
        )

    finish = ex(0, main, side)
    flat[...] = upstream[0].astype(F32).reshape(d.c * d.rows, d.cols)
    for r in range(d.rows):
        row = flat[pl.ds(r, d.c, stride=d.rows), :]
        cot[r] = (row * mask[...]).astype(BF16)
    finish()

    def start(g, at):
        return jnp.broadcast_to(offset[at, :][None], (d.rows, 8, d.cols))

    def store(g, at, acc):
        pre[:, at, :] = acc

    depthwise(d, main, side, taps, False, start, store)
    mlp(d, pre, cot, gain, shift, lift_t, lift, bias, drop, dmain, big_lift, big_drop, gain_acc, shift_acc)
    finish = ex(1, dmain, dside)
    taps_n = d.span * d.span
    lane = lanes((d.c, d.cols))
    small[...] = jnp.where(
        lane == taps_n + 1,
        jnp.sum(gain_acc[...], axis=1, keepdims=True),
        jnp.where(lane == taps_n + 2, jnp.sum(shift_acc[...], axis=1, keepdims=True), 0.0),
    )
    kernel_grads(d, main, side, dmain, small)
    finish()

    def start_back(g, at):
        return jnp.zeros((d.rows, 8, d.cols), F32)

    depthwise(d, dmain, dside, taps, True, start_back, store)
    for r in range(d.rows):
        flat[pl.ds(r, d.c, stride=d.rows), :] = mask[...] * (pre[r] + cot[r].astype(F32))
    out[0] = flat[...].reshape(d.c, d.rows, d.cols).astype(BF16)


def body(
    n,
    saved_input,
    tile_scale,
    ocean_tiles,
    upstream,
    kernel_taps,
    kernel_offset,
    norm_gain,
    norm_shift,
    lift_weight,
    lift_bias,
    drop_weight,
):
    channels, rows, cols = saved_input.shape[1:]
    hidden = lift_weight.shape[1]
    taps_n = kernel_taps.shape[0]
    d = Dims(n, channels, rows, cols, math.isqrt(taps_n), hidden)
    mask = jnp.repeat(ocean_tiles[0], rows).astype(F32)[None]
    scale = jnp.repeat(tile_scale[0].T, rows, axis=1) * mask
    taps = jnp.pad(kernel_taps.T, ((0, 0), (0, 128 - taps_n)))
    vmem = pl.BlockSpec(memory_space=pltpu.VMEM)
    grid3 = (d.ext, channels, cols)
    out, big_lift, big_drop, small = pl.pallas_call(
        functools.partial(kernel, d),
        out_shape=(
            jax.ShapeDtypeStruct((1, channels, rows, cols), BF16),
            jax.ShapeDtypeStruct((hidden, channels + 64), F32),
            jax.ShapeDtypeStruct((hidden, channels), F32),
            jax.ShapeDtypeStruct((channels, cols), F32),
        ),
        in_specs=[vmem] * 12,
        out_specs=(vmem,) * 4,
        scratch_shapes=[
            pltpu.VMEM((channels * rows, cols), F32),
            pltpu.VMEM(grid3, F32),
            pltpu.VMEM(grid3, F32),
            pltpu.VMEM(grid3, F32),
            pltpu.VMEM(grid3, F32),
            pltpu.VMEM((rows, channels, cols), BF16),
            pltpu.VMEM((rows, channels, cols), F32),
            pltpu.VMEM((2, 2, d.reach, channels, cols), BF16),
            pltpu.VMEM((2, 2, d.reach, channels, cols), BF16),
            pltpu.VMEM((2, channels, cols), BF16),
            pltpu.VMEM((2, 2, channels, cols), BF16),
            pltpu.VMEM((2, 2, 2, channels, cols), BF16),
            pltpu.VMEM((channels, cols), F32),
            pltpu.VMEM((channels, cols), F32),
            pltpu.SemaphoreType.DMA((2, 8)),
            pltpu.SemaphoreType.DMA((2, 8)),
        ],
        compiler_params=pltpu.CompilerParams(
            collective_id=0, has_side_effects=True, vmem_limit_bytes=56 * 1024 * 1024
        ),
        name="block_backward",
    )(
        saved_input,
        scale,
        mask,
        upstream,
        taps,
        kernel_offset[:, None],
        norm_gain[:, None],
        norm_shift[:, None],
        lift_weight.T,
        lift_weight,
        lift_bias[:, None],
        drop_weight,
    )
    big_lift, big_drop, small = lax.psum((big_lift, big_drop, small), "lon")
    factor = 1.0 / math.sqrt(n * rows * cols)
    small_t = small.T * factor
    return (
        out,
        small_t[:taps_n],
        small_t[taps_n],
        small_t[taps_n + 1],
        small_t[taps_n + 2],
        big_lift[:, :channels].T * factor,
        big_lift[:, channels] * factor,
        big_drop * factor,
    )


def solution(mesh):
    return jax.shard_map(
        functools.partial(body, mesh.shape["lon"]),
        mesh=mesh,
        in_specs=(
            P(("ens", "lon"), None, None, None),
            P(("ens", "lon"), None, None),
            P(("ens", "lon"), None),
            P(("ens", "lon"), None, None, None),
            P(),
            P(),
            P(),
            P(),
            P(),
            P(),
            P(),
        ),
        out_specs=(
            P(("ens", "lon"), None, None, None),
            P("ens", None),
            P("ens"),
            P("ens"),
            P("ens"),
            P("ens", None),
            P("ens"),
            P("ens", None),
        ),
        check_vma=False,
    )
```

time: 399 us -> 196 us (0.49)
  other arithmetic: 118 us -> 5.44 us
  matrix products: 86.8 us -> 0 us
  Pallas kernels: 0 us -> 64 us
  blocking collectives: 57.7 us -> 0 us
  waiting for transfers between devices: 71.3 us -> 97 us
  local copies, waits for them, and re-layouts: 30.7 us -> 14.7 us
  starting transfers between devices: 15.9 us -> 0.04 us
    dot_general x40 -> x0, matrix products: 86.8 us -> none  [the longest x8 21 us: mlp_backward(): jnp.dot(drop_weight, cotangent, preferred_element_type=jnp.float32)]
    pallas_call x0 -> x1, Pallas kernels: none -> 64 us  [body(): pl.pallas_call(functools.partial(kernel, d), out_shape=(jax.ShapeDtypeStr...]
    psum x1 -> x0, blocking collectives: 57.7 us -> none  [body(): lax.psum((lift_grad, drop_grad, bias_grad, gain_grad, shift_grad, kernel_...]
    reduce_sum x28 -> x0, other arithmetic: 39.9 us -> none  [the longest x3 18.3 us: conv_backward(): kernel_terms.append(jnp.sum(pre_grad * window, axis=(1, 2)))]
    psum x1, waiting for transfers between devices: 60.4 us -> 97 us  [body(): big_lift, big_drop, small = lax.psum((big_lift, big_drop, small), 'lon')]
    add x17 -> x0, other arithmetic: 32.6 us -> none  [the longest x1 22.1 us: depthwise(): total + weight * padded[:, tap_row:tap_row + tile_rows, tap_col:tap_col +...]
    broadcast_in_dim x2 -> x0, other arithmetic: 18.3 us -> none  [the longest x1 18.3 us: body(): (mask_cells * (cotangent.astype(jnp.float32) + conv_grad)).astype(jnp.bfl...]
    ppermute x8 -> x0, starting transfers between devices: 15.9 us -> none  [the longest x2 9.85 us: with_halo(): lax.ppermute(head, axis, [((i + 1) % count, i) for i in range(count)])]
  transfers between devices with their start and end apart: 9 -> 1, of which waited for: 6 -> 1; matrix products, arithmetic and copies ran while one was open for 8% -> 0% of each run, Pallas kernels for 0% -> 0%
where the time goes in v1:
time: 196 us; the launch traced here: 195 us
  waiting for transfers between devices  97 us (49%)
  Pallas kernels  64 us (33%)
  local copies, waits for them, and re-layouts  14.7 us (8%)
  between operations  14.1 us (7%)
  other arithmetic  5.44 us (3%)
    psum x1, waiting for transfers between devices, body(): big_lift, big_drop, small = lax.psum((big_lift, big_drop, small), 'lon')  97 us
    pallas_call x1, Pallas kernels, body(): pl.pallas_call(functools.partial(kernel, d), out_shape=(jax.ShapeDtypeStr...  64 us
    unnamed x25, local copies, waits for them, and re-layouts  9.14 us
  transfers between devices with their start and end apart: 1, of which 1 were waited for; matrix products, arithmetic and copies ran while one was open for 0% of the time, Pallas kernels for 0%

profile of v1, /device:TPU:0, one launch (start us, length us, event | category | flops | bytes accessed | tf_op | source)
XLA Modules:
  0.0 195.2 jit_solution(10092477129451216924)
XLA Ops:
  7.2 0.0 all-reduce.4.cloned.1.call-start
  7.2 0.7 convert_bitcast_fusion
  7.9 0.1 broadcast_in_dim.20
  7.9 0.6 convert_element_type.28.mask
  8.5 0.1 convert_element_type.27
  8.6 0.9 copy.27
  9.5 0.7 copy-done.6
  10.2 0.8 copy.29.offset
  11.0 0.7 copy-done.7
  11.7 0.8 copy.30.gain
  12.4 0.7 copy-done.8
  13.1 0.8 copy.31.shift
  13.9 0.0 copy-start.3
  13.9 0.1 copy.26
  14.0 0.6 copy-done.5
  14.6 0.9 broadcast_in_dim.25.bias
  15.5 0.9 copy.33.drop
  16.4 0.0 copy-done.1
  16.4 0.9 copy.28
  17.4 0.7 pad.4.taps
  18.0 0.6 broadcast_multiply_fusion.1.scale
  18.7 64.0 %block_backward.1 = (bf16[1,192,16,128]{3,2,1,0:T(8,128)(2,1)}, f32[768,256]{1,0:T(8,128)}, f32[768,192]{1,0:T(8,128)}, f32[192,128]{1,0:T(8,128)}) custom-call(bf16[1,192,16,128]{3,2,1,0:T(8,128)(2,1)} %saved.1, f32[192,128]{1,0:T(8,128)} %broadcast_multiply_fusion.1.scale, f32[1,128]{1,0:T(1,128)} %convert_element_type.28.mask, ...), custom_call_target="tpu_custom_call" | custom-call | tf_op jit(solution)/shard_map/block_backward/pallas_call | solution.py:334
  82.6 0.0 all-reduce.4.cloned.1.call-update
  82.7 97.0 %all-reduce.4.cloned.1.call-done = (f32[192,128]{1,0:T(8,128)}, f32[768,256]{1,0:T(8,128)}, f32[768,192]{1,0:T(8,128)}) async-done(((f32[192,128]{1,0:T(8,128)}, f32[768,256]{1,0:T(8,128)}, f32[768,192]{1,0:T(8,128)}), (f32[192,128]{1,0:T(8,128)}, f32[768,256]{1,0:T(8,128)}, f32[768,192]{1,0:T(8,128)})) %all-reduce.4.cloned.1.call-update) | async-done | bytes 1474576 | tf_op jit(solution)/shard_map/psum | solution.py:380
  179.6 1.0 multiply_bitcast_fusion
  180.6 0.9 slice_reduce_fusion
  181.5 1.9 fusion.1
  183.4 1.3 fusion
  184.6 1.1 copy.35
  185.7 0.7 copy.34
  186.4 1.1 copy.36
  187.5 0.9 copy.41
  (13 shorter events, 0.0 us)
Async XLA Ops:
  7.2 172.4 %all-reduce.4.cloned.1.call-start = ((), (), s32[]{:S(2)}) async-start(), calls=%async_computation | async-start | bytes 3342336 | tf_op jit(solution)/shard_map/psum | solution.py:380
  9.5 0.7 copy-start.6
  11.0 0.7 copy-start.7
  12.4 0.7 copy-start.8
  13.1 0.8 copy-start.4
  13.9 0.7 copy-start.5
  13.9 1.6 copy-start.3
  15.5 1.0 copy-start.1
  179.6 3.7 %copy-start = (f32[768,256]{1,0:T(8,128)S(1)}, f32[768,256]{1,0:T(8,128)}, u32[]{:S(2)}) copy-start(f32[768,256]{1,0:T(8,128)} %get-tuple-element.36) | copy-start | bytes 2359300
  185.7 1.8 copy-start.2
Sparse Core Ops, SparseCore 0:
  82.8 96.7 all-reduce.3

commit v2 on v1

--- a/solution.py
+++ b/solution.py
@@ -30,6 +30,7 @@
         self.span, self.reach = span, span // 2
         self.ext = rows + 2 * self.reach
         self.same = 2 * LAT_DEVS == n
+        self.group = 2 * LAT_DEVS
 
 
 def neighbours(d):
@@ -156,7 +157,7 @@
     return roll(jnp.where(keep, h, x), -s)
 
 
-def depthwise(d, main, side, taps, flip, start, store):
+def depthwise(d, main, side, taps, flip, start, store, first, last):
     def group(g, carry):
         at = pl.ds(pl.multiple_of(g * 8, 8), 8)
         weights = taps[at, :]
@@ -171,7 +172,7 @@
         store(g, at, acc)
         return carry
 
-    lax.fori_loop(0, d.c // 8, group, 0)
+    lax.fori_loop(first, last, group, 0)
 
 
 def kernel_grads(d, main, side, dmain, small):
@@ -198,7 +199,7 @@
     return lax.dot_general(a, b, (dims, ((), ())), preferred_element_type=F32)
 
 
-def mlp(d, pre, cot, gain, shift, lift_t, lift, bias, drop, dmain, big_lift, big_drop, gain_acc, shift_acc):
+def mlp(d, pre, cot, columns, lift_t, lift, drop, dmain, big_lift, big_drop, gain_acc, shift_acc):
     step_rows = 4
     block = 256
     wide = step_rows * d.cols
@@ -207,6 +208,9 @@
     big_drop[...] = jnp.zeros_like(big_drop)
     gain_acc[...] = jnp.zeros_like(gain_acc)
     shift_acc[...] = jnp.zeros_like(shift_acc)
+    at = d.span * d.span
+    gain = columns[: d.c, at + 1 : at + 2]
+    shift = columns[: d.c, at + 2 : at + 3]
 
     def fold(x):
         return sum(x[:, j * d.cols : (j + 1) * d.cols] for j in range(step_rows))
@@ -218,27 +222,29 @@
         centre = x - jnp.mean(x, axis=0, keepdims=True)
         inverse = lax.rsqrt(jnp.mean(centre * centre, axis=0, keepdims=True) + EPSILON)
         normed = centre * inverse
-        lifted = (normed * gain[...] + shift[...]).astype(BF16)
+        lifted = (normed * gain + shift).astype(BF16)
         ones = jnp.where(
             lax.broadcasted_iota(jnp.int32, (64, wide), 0) == 0, 1.0, 0.0
         ).astype(BF16)
         lifted_one = jnp.concatenate([lifted, ones], axis=0)
+        gap = jnp.zeros((64, wide), BF16)
+        ct_apart = jnp.concatenate([ct[:128], gap, ct[128:]], axis=0)
         lifted_grad = jnp.zeros((d.c, wide), F32)
         for b in range(d.hidden // block):
             hs = slice(b * block, (b + 1) * block)
-            v = dot(lift_t[hs, :], lifted) + bias[hs, :]
+            v = dot(lift_t[hs, :], lifted) + columns[:, at + 3 + b : at + 4 + b]
             act_grad = dot(drop[hs, :], ct)
             v2 = v * v
             half = 0.5 * jnp.tanh(v * (root + (root * 0.044715) * v2)) + 0.5
             act = v * half
             slope = half + (act * (1.0 - half)) * (2.0 * root + (6.0 * root * 0.044715) * v2)
             hidden_round = (act_grad * slope).astype(BF16)
-            big_drop[hs, :] += dot(act.astype(BF16), ct, ((1,), (1,)))
+            big_drop[hs, :] += dot(act.astype(BF16), ct_apart, ((1,), (1,)))
             big_lift[hs, :] += dot(hidden_round, lifted_one, ((1,), (1,)))
             lifted_grad = lifted_grad + dot(lift[:, hs], hidden_round)
         gain_acc[...] += fold(lifted_grad * normed)
         shift_acc[...] += fold(lifted_grad)
-        ng = lifted_grad * gain[...]
+        ng = lifted_grad * gain
         m1 = jnp.mean(ng, axis=0, keepdims=True)
         m2 = jnp.mean(ng * normed, axis=0, keepdims=True)
         pg = (inverse * (ng - m1 - normed * m2)).astype(BF16).astype(F32)
@@ -249,22 +255,179 @@
     lax.fori_loop(0, d.rows // step_rows, step, 0)
 
 
+def remote(src, dst, ssem, rsem, peer):
+    return pltpu.make_async_remote_copy(
+        src_ref=src,
+        dst_ref=dst,
+        send_sem=ssem,
+        recv_sem=rsem,
+        device_id={"lon": peer},
+        device_id_type=MESH,
+    )
+
+
+class Sums:
+    def __init__(self, d, bufs, factor):
+        self.d, self.factor = d, factor
+        (self.mine, self.from_core, self.pair, self.from_chip, self.all, self.small, self.small_in,
+         self.small_all, self.csem, self.hsem, self.gsem, self.dsem, self.rsem, self.asem) = bufs
+        me = lax.axis_index("lon")
+        self.chips = d.group // 2
+        self.rank = lax.rem(me, d.group)
+        self.base = me - self.rank
+        self.core = lax.rem(self.rank, 2)
+        self.chip = self.rank // 2
+        self.partner = self.base + self.chip * 2 + (1 - self.core)
+
+    def chip_peer(self, t):
+        other = lax.rem(self.chip + t, self.chips)
+        return other, self.base + other * 2 + self.core
+
+    def start_pair(self, big_lift, big_drop):
+        chunk = self.mine.shape[2]
+        lane = lanes((chunk, 128))
+        for h in range(2):
+            for c in range(self.chips):
+                at = slice((h * self.chips + c) * chunk, (h * self.chips + c + 1) * chunk)
+                middle = jnp.where(lane < 64, big_lift[at, 128:], big_drop[at, 128:])
+                self.mine[h, c, :, 0:128] = big_lift[at, :128].astype(BF16)
+                self.mine[h, c, :, 128:256] = middle.astype(BF16)
+                self.mine[h, c, :, 256:384] = big_drop[at, :128].astype(BF16)
+        self.pair_copy = remote(
+            self.mine.at[1 - self.core], self.from_core, self.csem.at[0], self.csem.at[1], self.partner
+        )
+        self.pair_copy.start()
+
+    def start_chips(self):
+        self.pair_copy.wait()
+        for c in range(self.chips):
+            self.pair[c] = (self.mine[self.core, c].astype(F32) + self.from_core[c].astype(F32)).astype(BF16)
+        self.chip_copies = []
+        for t in range(1, self.chips):
+            other, peer = self.chip_peer(t)
+            self.chip_copies.append(
+                remote(self.pair.at[other], self.from_chip.at[t - 1], self.hsem.at[0, t], self.hsem.at[1, t], peer)
+            )
+        for one in self.chip_copies:
+            one.start()
+
+    def start_gather(self):
+        for one in self.chip_copies:
+            one.wait()
+        total = self.pair[self.chip].astype(F32)
+        for t in range(1, self.chips):
+            total = total + self.from_chip[t - 1].astype(F32)
+        self.all[self.core, self.chip] = (total * self.factor).astype(BF16)
+        self.gathers = []
+        for t in range(1, self.chips):
+            other, peer = self.chip_peer(t)
+            place = self.all.at[self.core, self.chip]
+            self.gathers.append(remote(place, place, self.gsem.at[0, t], self.gsem.at[1, t], peer))
+        for one in self.gathers:
+            one.start()
+
+    def start_back(self):
+        for one in self.gathers:
+            one.wait()
+        half = self.all.at[self.core]
+        self.back = remote(half, half, self.dsem.at[0], self.dsem.at[1], self.partner)
+        self.back.start()
+
+    def finish(self, out_lift, out_drop):
+        self.back.wait()
+        rows = self.chips * self.mine.shape[2]
+        for h in range(2):
+            at = slice(h * rows, (h + 1) * rows)
+            part = self.all[h].reshape(rows, 384).astype(F32)
+            middle = part[:, 128:256]
+            out_drop[at, 0:128] = part[:, 256:]
+            out_drop[at, 128:192] = roll(middle, 64)[:, :64]
+            out_lift[0:128, at] = part[:, :128].T
+            out_lift[128:192, at] = middle.T[:64]
+
+    def start_small(self):
+        self.small_copies = []
+        for t in range(1, self.d.group):
+            other = lax.rem(self.rank + t, self.d.group)
+            self.small_copies.append(
+                remote(self.small.at[other], self.small_in.at[t - 1], self.rsem.at[0, t], self.rsem.at[1, t], self.base + other)
+            )
+        for one in self.small_copies:
+            one.start()
+
+    def start_small_gather(self):
+        for one in self.small_copies:
+            one.wait()
+        total = self.small[self.rank]
+        for t in range(1, self.d.group):
+            total = total + self.small_in[t - 1]
+        self.small_all[self.rank] = total * self.factor
+        self.small_copies = []
+        for t in range(1, self.d.group):
+            other = lax.rem(self.rank + t, self.d.group)
+            place = self.small_all.at[self.rank]
+            self.small_copies.append(
+                remote(place, place, self.asem.at[0, t], self.asem.at[1, t], self.base + other)
+            )
+        for one in self.small_copies:
+            one.start()
+
+    def finish_small(self):
+        for one in self.small_copies:
+            one.wait()
+        return self.small_all[...].reshape(128, 128)
+
+
 def kernel(
-    d,
-    saved, scale, mask, upstream, taps, offset, gain, shift, lift_t, lift, bias, drop,
-    out, big_lift, big_drop, small,
+    d, factor,
+    saved, tile_scale, ocean, upstream, taps, offset, gain, shift, lift, bias, drop,
+    out, out_taps, out_offset, out_gain, out_shift, out_lift, out_bias, out_drop,
     flat, main, side, dmain, dside, cot, pre, rows_out, rows_in, pack_out, pack_in, fwd_in,
-    gain_acc, shift_acc, ssem, rsem,
+    gain_acc, shift_acc, ssem, rsem, columns, lift_t, big_lift, big_drop, small_cols, *bufs,
 ):
     me, north, south, east, west = neighbours(d)
-    peers = [north, south, west] if d.same else [north, south, west, east]
+    sums = Sums(d, bufs, factor)
+    peers = [sums.base + lax.rem(sums.rank + t, d.group) for t in range(1, d.group)]
+    if d.n != d.group:
+        peers += [north, south, east, west]
     barrier = pltpu.get_barrier_semaphore()
     for peer in peers:
         pl.semaphore_signal(barrier, inc=1, device_id={"lon": peer}, device_id_type=MESH)
+    taps_n = d.span * d.span
+    wide = 256
+    blocks = d.hidden // wide
+    slots = tile_scale.shape[1]
+    pad = jnp.zeros((1, wide - d.c), F32)
+
+    def widen(x):
+        return jnp.concatenate([x, jnp.broadcast_to(pad, (x.shape[0], wide - d.c))], axis=1)
+
+    rows = flat.at[0:256]
+    rows[...] = jnp.zeros_like(rows)
+    for h, (lo, hi) in enumerate(((0, 128), (128, d.c))):
+        at = slice(h * 128, h * 128 + taps_n)
+        rows[at, 0 : hi - lo] = taps[:, lo:hi]
+        for k, one in enumerate((offset, gain, shift)):
+            rows[h * 128 + taps_n + k : h * 128 + taps_n + k + 1, 0 : hi - lo] = one[:, lo:hi]
+        for b in range(blocks):
+            rows[h * 128 + taps_n + 3 + b : h * 128 + taps_n + 4 + b, :] = bias[
+                :, b * wide + h * 128 : b * wide + h * 128 + 128
+            ]
+        rows[h * 128 + 56 : h * 128 + 56 + slots, 0 : hi - lo] = tile_scale[0, :, lo:hi]
+        columns[h * 128 : h * 128 + 128, :] = rows[h * 128 : h * 128 + 128, :].T
+    lane = lanes((1, d.cols))
+    mask = jnp.zeros((1, d.cols), F32)
+    scale = jnp.zeros((d.c, d.cols), F32)
+    for s in range(slots):
+        here = (lane >= s * d.rows) & (lane < (s + 1) * d.rows)
+        mask = jnp.where(here, ocean[:, s : s + 1].astype(F32), mask)
+        scale = jnp.where(here, columns[: d.c, 56 + s : 57 + s], scale)
+    scale = scale * mask
+    lift_t[...] = lift[...].astype(F32).T.astype(BF16)
     flat[...] = saved[0].astype(F32).reshape(d.c * d.rows, d.cols)
     for r in range(d.rows):
         row = flat[pl.ds(r, d.c, stride=d.rows), :]
-        main[d.reach + r] = (row * scale[...]).astype(BF16).astype(F32)
+        main[d.reach + r] = (row * scale).astype(BF16).astype(F32)
     pl.semaphore_wait(barrier, len(peers))
 
     def ex(i, m, s):
@@ -277,35 +440,64 @@
     flat[...] = upstream[0].astype(F32).reshape(d.c * d.rows, d.cols)
     for r in range(d.rows):
         row = flat[pl.ds(r, d.c, stride=d.rows), :]
-        cot[r] = (row * mask[...]).astype(BF16)
+        cot[r] = (row * mask).astype(BF16)
     finish()
 
     def start(g, at):
-        return jnp.broadcast_to(offset[at, :][None], (d.rows, 8, d.cols))
+        return jnp.broadcast_to(columns[at, taps_n : taps_n + 1][None], (d.rows, 8, d.cols))
 
     def store(g, at, acc):
         pre[:, at, :] = acc
 
-    depthwise(d, main, side, taps, False, start, store)
-    mlp(d, pre, cot, gain, shift, lift_t, lift, bias, drop, dmain, big_lift, big_drop, gain_acc, shift_acc)
+    groups = d.c // 8
+    depthwise(d, main, side, columns, False, start, store, 0, groups)
+    mlp(d, pre, cot, columns, lift_t, lift, drop, dmain, big_lift, big_drop, gain_acc, shift_acc)
     finish = ex(1, dmain, dside)
-    taps_n = d.span * d.span
+    sums.start_pair(big_lift, big_drop)
     lane = lanes((d.c, d.cols))
-    small[...] = jnp.where(
+    small_cols[...] = jnp.zeros_like(small_cols)
+    small_cols[: d.c, :] = jnp.where(
         lane == taps_n + 1,
         jnp.sum(gain_acc[...], axis=1, keepdims=True),
         jnp.where(lane == taps_n + 2, jnp.sum(shift_acc[...], axis=1, keepdims=True), 0.0),
     )
-    kernel_grads(d, main, side, dmain, small)
+    kernel_grads(d, main, side, dmain, small_cols)
+    lane = lanes((wide, d.cols))
+    for b in range(blocks):
+        column = big_lift[b * wide : (b + 1) * wide, d.c : d.c + 1]
+        small_cols[...] = jnp.where(lane == taps_n + 3 + b, column, small_cols[...])
+    for h in range(2):
+        turned = small_cols[h * 128 : h * 128 + 128, :].T
+        for i in range(8):
+            sums.small[h * 8 + i] = turned[i * 8 : i * 8 + 8]
+    sums.start_chips()
+    sums.start_small()
     finish()
 
     def start_back(g, at):
         return jnp.zeros((d.rows, 8, d.cols), F32)
 
-    depthwise(d, dmain, dside, taps, True, start_back, store)
+    third = groups // 3
+    depthwise(d, dmain, dside, columns, True, start_back, store, 0, third)
+    sums.start_gather()
+    sums.start_small_gather()
+    depthwise(d, dmain, dside, columns, True, start_back, store, third, 2 * third)
+    sums.start_back()
+    depthwise(d, dmain, dside, columns, True, start_back, store, 2 * third, groups)
     for r in range(d.rows):
-        flat[pl.ds(r, d.c, stride=d.rows), :] = mask[...] * (pre[r] + cot[r].astype(F32))
+        flat[pl.ds(r, d.c, stride=d.rows), :] = mask * (pre[r] + cot[r].astype(F32))
     out[0] = flat[...].reshape(d.c, d.rows, d.cols).astype(BF16)
+    small = sums.finish_small()
+    for h, (lo, hi) in enumerate(((0, 128), (128, d.c))):
+        base = h * 64
+        out_taps[:, lo:hi] = small[base : base + taps_n, 0 : hi - lo]
+        for k, one in enumerate((out_offset, out_gain, out_shift)):
+            one[:, lo:hi] = small[base + taps_n + k : base + taps_n + k + 1, 0 : hi - lo]
+        for b in range(blocks):
+            out_bias[:, b * wide + h * 128 : b * wide + h * 128 + 128] = small[
+                base + taps_n + 3 + b : base + taps_n + 4 + b
+            ]
+    sums.finish(out_lift, out_drop)
 
 
 def body(
@@ -326,21 +518,26 @@
     hidden = lift_weight.shape[1]
     taps_n = kernel_taps.shape[0]
     d = Dims(n, channels, rows, cols, math.isqrt(taps_n), hidden)
-    mask = jnp.repeat(ocean_tiles[0], rows).astype(F32)[None]
-    scale = jnp.repeat(tile_scale[0].T, rows, axis=1) * mask
-    taps = jnp.pad(kernel_taps.T, ((0, 0), (0, 128 - taps_n)))
     vmem = pl.BlockSpec(memory_space=pltpu.VMEM)
     grid3 = (d.ext, channels, cols)
-    out, big_lift, big_drop, small = pl.pallas_call(
-        functools.partial(kernel, d),
+    factor = 1.0 / math.sqrt(n * rows * cols)
+    chips = d.group // 2
+    chunk = hidden // d.group
+    dma = pltpu.SemaphoreType.DMA
+    out, *grads = pl.pallas_call(
+        functools.partial(kernel, d, factor),
         out_shape=(
             jax.ShapeDtypeStruct((1, channels, rows, cols), BF16),
-            jax.ShapeDtypeStruct((hidden, channels + 64), F32),
+            jax.ShapeDtypeStruct((taps_n, channels), F32),
+            jax.ShapeDtypeStruct((1, channels), F32),
+            jax.ShapeDtypeStruct((1, channels), F32),
+            jax.ShapeDtypeStruct((1, channels), F32),
+            jax.ShapeDtypeStruct((channels, hidden), F32),
+            jax.ShapeDtypeStruct((1, hidden), F32),
             jax.ShapeDtypeStruct((hidden, channels), F32),
-            jax.ShapeDtypeStruct((channels, cols), F32),
         ),
-        in_specs=[vmem] * 12,
-        out_specs=(vmem,) * 4,
+        in_specs=[vmem] * 11,
+        out_specs=(vmem,) * 8,
         scratch_shapes=[
             pltpu.VMEM((channels * rows, cols), F32),
             pltpu.VMEM(grid3, F32),
@@ -356,8 +553,27 @@
             pltpu.VMEM((2, 2, 2, channels, cols), BF16),
             pltpu.VMEM((channels, cols), F32),
             pltpu.VMEM((channels, cols), F32),
-            pltpu.SemaphoreType.DMA((2, 8)),
-            pltpu.SemaphoreType.DMA((2, 8)),
+            dma((2, 8)),
+            dma((2, 8)),
+            pltpu.VMEM((256, 128), F32),
+            pltpu.VMEM((hidden, channels), BF16),
+            pltpu.VMEM((hidden, 256), F32),
+            pltpu.VMEM((hidden, 256), F32),
+            pltpu.VMEM((256, 128), F32),
+            pltpu.VMEM((2, chips, chunk, 384), BF16),
+            pltpu.VMEM((chips, chunk, 384), BF16),
+            pltpu.VMEM((chips, chunk, 384), BF16),
+            pltpu.VMEM((chips - 1, chunk, 384), BF16),
+            pltpu.VMEM((2, chips, chunk, 384), BF16),
+            pltpu.VMEM((d.group, 8, 128), F32),
+            pltpu.VMEM((d.group - 1, 8, 128), F32),
+            pltpu.VMEM((d.group, 8, 128), F32),
+            dma((2,)),
+            dma((2, chips)),
+            dma((2, chips)),
+            dma((2,)),
+            dma((2, d.group)),
+            dma((2, d.group)),
         ],
         compiler_params=pltpu.CompilerParams(
             collective_id=0, has_side_effects=True, vmem_limit_bytes=56 * 1024 * 1024
@@ -365,31 +581,22 @@
         name="block_backward",
     )(
         saved_input,
-        scale,
-        mask,
+        tile_scale,
+        ocean_tiles,
         upstream,
-        taps,
-        kernel_offset[:, None],
-        norm_gain[:, None],
-        norm_shift[:, None],
-        lift_weight.T,
+        kernel_taps,
+        kernel_offset[None],
+        norm_gain[None],
+        norm_shift[None],
         lift_weight,
-        lift_bias[:, None],
+        lift_bias[None],
         drop_weight,
     )
-    big_lift, big_drop, small = lax.psum((big_lift, big_drop, small), "lon")
-    factor = 1.0 / math.sqrt(n * rows * cols)
-    small_t = small.T * factor
-    return (
-        out,
-        small_t[:taps_n],
-        small_t[taps_n],
-        small_t[taps_n + 1],
-        small_t[taps_n + 2],
-        big_lift[:, :channels].T * factor,
-        big_lift[:, channels] * factor,
-        big_drop * factor,
-    )
+    if n != d.group:
+        across = [[i + d.group * k for k in range(n // d.group)] for i in range(d.group)]
+        grads = lax.psum(grads, "lon", axis_index_groups=across)
+    g_taps, g_offset, g_gain, g_shift, g_lift, g_bias, g_drop = grads
+    return (out, g_taps, g_offset[0], g_gain[0], g_shift[0], g_lift, g_bias[0], g_drop)
 
 
 def solution(mesh):

time: 196 us -> 86.1 us (0.44)
  waiting for transfers between devices: 97 us -> 0 us
  between operations: 14.1 us -> 0.67 us
  Pallas kernels: 64 us -> 74.2 us
  local copies, waits for them, and re-layouts: 14.7 us -> 9.51 us
  other arithmetic: 5.44 us -> 1.36 us
    psum x1 -> x0, waiting for transfers between devices: 97 us -> none  [body(): big_lift, big_drop, small = lax.psum((big_lift, big_drop, small), 'lon')]
    pallas_call x1, Pallas kernels: 64 us -> 74.2 us  [body(): pl.pallas_call(functools.partial(kernel, d, factor), out_shape=(jax.Shape...]
    mul x4 -> x0, other arithmetic: 4.78 us -> none  [the longest x1 1.89 us: body(): big_lift[:, channels] * factor]
    broadcast_in_dim x6 -> x1, local copies, waits for them, and re-layouts: 3.28 us -> 0.58 us  [body(): lift_bias[None]]
    unnamed x25 -> x22, local copies, waits for them, and re-layouts: 9.14 us -> 8.93 us
  transfers between devices with their start and end apart: 1 -> 0, of which waited for: 1 -> 0; matrix products, arithmetic and copies ran while one was open for 0% -> 0% of each run, Pallas kernels for 0% -> 0%
where the time goes in v2:
time: 86.1 us; the launch traced here: 85.7 us
  Pallas kernels  74.2 us (86%)
  local copies, waits for them, and re-layouts  9.51 us (11%)
  other arithmetic  1.36 us (2%)
    pallas_call x1, Pallas kernels, body(): pl.pallas_call(functools.partial(kernel, d, factor), out_shape=(jax.Shape...  74.2 us
    unnamed x22, local copies, waits for them, and re-layouts  8.93 us

profile of v2, /device:TPU:0, one launch (start us, length us, event | category | flops | bytes accessed | tf_op | source)
XLA Modules:
  0.0 85.7 jit_solution(15564271055874073488)
XLA Ops:
  0.6 0.0 copy-start.3
  0.6 0.7 copy-done.3
  1.3 0.6 broadcast_in_dim.15.bias
  1.9 1.9 %copy.19.drop = bf16[768,192]{1,0:T(8,128)(2,1)} copy(bf16[768,192]{0,1:T(8,128)(2,1)} %param.21) | data formatting | bytes 589824 | tf_op args[10]
  3.8 74.2 %block_backward.1 = (bf16[1,192,16,128]{3,2,1,0:T(8,128)(2,1)}, f32[49,192]{1,0:T(8,128)}, f32[1,192]{1,0:T(1,128)}, f32[1,192]{1,0:T(1,128)}, f32[1,192]{1,0:T(...) custom-call(bf16[1,192,16,128]{3,2,1,0:T(8,128)(2,1)} %saved.1, f32[1,8,192]{2,1,0:T(8,128)} %tile_scale.1, ...), custom_call_target="tpu_custom_call" | custom-call | tf_op jit(solution)/shard_map/block_backward/pallas_call | solution.py:527
  78.0 0.0 copy-start
  78.0 1.4 %reduce = f32[768]{0:T(1024)} reduce(f32[1,768]{1,0:T(1,128)} %get-tuple-element.22, f32[]{:T(128)} %constant.4), dimensions={0}, to_apply=%get-tuple-element.22.reduce_sub_computation | reduce | bytes 6148 | tf_op jit(solution)/shard_map/block_backward/pallas_call | solution.py:527
  79.3 2.2 %copy.20 = f32[768,192]{0,1:T(8,128)} copy(f32[768,192]{1,0:T(8,128)} %get-tuple-element.31) | data formatting | bytes 1179648
  81.5 0.0 copy-done
  81.5 0.0 copy-start.2
  81.5 0.0 copy-start.1
  81.6 0.9 %copy.27 = bf16[1,192,16,128]{3,2,1,0:T(8,128)(2,1)} copy(bf16[1,192,16,128]{3,2,1,0:T(8,128)(2,1)S(1)} %copy-done) | data formatting | bytes 1572864
  82.4 0.0 copy-done.2
  82.4 0.0 copy-start.6
  82.4 0.6 copy.28
  83.1 0.0 copy-done.6
  83.1 0.0 copy-start.5
  83.1 0.6 copy.29
  83.6 0.0 copy-done.5
  83.7 0.0 copy-start.4
  83.7 0.6 copy.30
  84.2 0.1 copy-done.4
  84.3 0.6 copy.31
  84.9 0.0 copy-done.1
  84.9 0.8 copy.32
Async XLA Ops:
  0.6 0.7 copy-start.3
  78.0 3.6 %copy-start = (bf16[1,192,16,128]{3,2,1,0:T(8,128)(2,1)S(1)}, bf16[1,192,16,128]{3,2,1,0:T(8,128)(2,1)}, u32[]{:S(2)}) copy-start(bf16[1,192,16,128]{3,2,1,0:T(8,128)(2,1)} %get-tuple-element.40) | copy-start | bytes 2359300
  81.5 0.9 %copy-start.2 = (f32[49,192]{1,0:T(8,128)S(1)}, f32[49,192]{1,0:T(8,128)}, u32[]{:S(2)}) copy-start(f32[49,192]{1,0:T(8,128)} %get-tuple-element.41) | copy-start | bytes 112900
  81.5 3.4 %copy-start.1 = (f32[192,768]{1,0:T(8,128)S(1)}, f32[192,768]{1,0:T(8,128)}, u32[]{:S(2)}) copy-start(f32[192,768]{1,0:T(8,128)} %get-tuple-element.45) | copy-start | bytes 1769476
  82.4 0.6 copy-start.6
  83.1 0.6 copy-start.5
  83.7 0.7 copy-start.4

commit v3 on v2

--- a/solution.py
+++ b/solution.py
@@ -340,10 +340,11 @@
             at = slice(h * rows, (h + 1) * rows)
             part = self.all[h].reshape(rows, 384).astype(F32)
             middle = part[:, 128:256]
-            out_drop[at, 0:128] = part[:, 256:]
-            out_drop[at, 128:192] = roll(middle, 64)[:, :64]
+            turned = middle.T
+            out_drop[0:128, at] = part[:, 256:].T
+            out_drop[128:192, at] = turned[64:]
             out_lift[0:128, at] = part[:, :128].T
-            out_lift[128:192, at] = middle.T[:64]
+            out_lift[128:192, at] = turned[:64]
 
     def start_small(self):
         self.small_copies = []
@@ -383,7 +384,7 @@
     saved, tile_scale, ocean, upstream, taps, offset, gain, shift, lift, bias, drop,
     out, out_taps, out_offset, out_gain, out_shift, out_lift, out_bias, out_drop,
     flat, main, side, dmain, dside, cot, pre, rows_out, rows_in, pack_out, pack_in, fwd_in,
-    gain_acc, shift_acc, ssem, rsem, columns, lift_t, big_lift, big_drop, small_cols, *bufs,
+    gain_acc, shift_acc, ssem, rsem, columns, lift_t, drop_t, big_lift, big_drop, small_cols, *bufs,
 ):
     me, north, south, east, west = neighbours(d)
     sums = Sums(d, bufs, factor)
@@ -424,6 +425,7 @@
         scale = jnp.where(here, columns[: d.c, 56 + s : 57 + s], scale)
     scale = scale * mask
     lift_t[...] = lift[...].astype(F32).T.astype(BF16)
+    drop_t[...] = drop[...].astype(F32).T.astype(BF16)
     flat[...] = saved[0].astype(F32).reshape(d.c * d.rows, d.cols)
     for r in range(d.rows):
         row = flat[pl.ds(r, d.c, stride=d.rows), :]
@@ -451,7 +453,7 @@
 
     groups = d.c // 8
     depthwise(d, main, side, columns, False, start, store, 0, groups)
-    mlp(d, pre, cot, columns, lift_t, lift, drop, dmain, big_lift, big_drop, gain_acc, shift_acc)
+    mlp(d, pre, cot, columns, lift_t, lift, drop_t, dmain, big_lift, big_drop, gain_acc, shift_acc)
     finish = ex(1, dmain, dside)
     sums.start_pair(big_lift, big_drop)
     lane = lanes((d.c, d.cols))
@@ -534,7 +536,7 @@
             jax.ShapeDtypeStruct((1, channels), F32),
             jax.ShapeDtypeStruct((channels, hidden), F32),
             jax.ShapeDtypeStruct((1, hidden), F32),
-            jax.ShapeDtypeStruct((hidden, channels), F32),
+            jax.ShapeDtypeStruct((channels, hidden), F32),
         ),
         in_specs=[vmem] * 11,
         out_specs=(vmem,) * 8,
@@ -556,6 +558,7 @@
             dma((2, 8)),
             dma((2, 8)),
             pltpu.VMEM((256, 128), F32),
+            pltpu.VMEM((hidden, channels), BF16),
             pltpu.VMEM((hidden, channels), BF16),
             pltpu.VMEM((hidden, 256), F32),
             pltpu.VMEM((hidden, 256), F32),
@@ -590,13 +593,13 @@
         norm_shift[None],
         lift_weight,
         lift_bias[None],
-        drop_weight,
+        drop_weight.T,
     )
     if n != d.group:
         across = [[i + d.group * k for k in range(n // d.group)] for i in range(d.group)]
         grads = lax.psum(grads, "lon", axis_index_groups=across)
     g_taps, g_offset, g_gain, g_shift, g_lift, g_bias, g_drop = grads
-    return (out, g_taps, g_offset[0], g_gain[0], g_shift[0], g_lift, g_bias[0], g_drop)
+    return (out, g_taps, g_offset[0], g_gain[0], g_shift[0], g_lift, g_bias.reshape(-1), g_drop.T)
 
 
 def solution(mesh):

time: 86.1 us -> 84.5 us (0.981)
    unnamed x22 -> x23, local copies, waits for them, and re-layouts: 8.93 us -> 8.2 us
where the time goes in v3:
time: 84.5 us; the launch traced here: 84.2 us
  Pallas kernels  74.1 us (88%)
  local copies, waits for them, and re-layouts  8.78 us (10%)
    pallas_call x1, Pallas kernels, body(): pl.pallas_call(functools.partial(kernel, d, factor), out_shape=(jax.Shape...  74.1 us
    unnamed x23, local copies, waits for them, and re-layouts  8.2 us

profile of v3, /device:TPU:0, one launch (start us, length us, event | category | flops | bytes accessed | tf_op | source)
XLA Modules:
  0.0 84.2 jit_solution(15092967469443274127)
XLA Ops:
  0.6 0.0 copy-start.3
  0.6 0.7 copy-done.3
  1.3 0.6 broadcast_in_dim.15.bias
  1.9 74.1 %block_backward.1 = (bf16[1,192,16,128]{3,2,1,0:T(8,128)(2,1)}, f32[49,192]{1,0:T(8,128)}, f32[1,192]{1,0:T(1,128)}, f32[1,192]{1,0:T(1,128)}, f32[1,192]{1,0:T(...) custom-call(bf16[1,192,16,128]{3,2,1,0:T(8,128)(2,1)} %saved.1, f32[1,8,192]{2,1,0:T(8,128)} %tile_scale.1, ...), custom_call_target="tpu_custom_call" | custom-call | tf_op jit(solution)/shard_map/block_backward/pallas_call | solution.py:529
  76.1 0.0 copy-start.4
  76.1 0.7 copy-done.4
  76.7 0.6 reduce
  77.3 0.0 copy-start.2
  77.3 0.0 copy-start.1
  77.3 2.2 %copy.26 = bf16[1,192,16,128]{3,2,1,0:T(8,128)(2,1)} copy(bf16[1,192,16,128]{3,2,1,0:T(8,128)(2,1)} %get-tuple-element.32) | data formatting | bytes 1572864
  79.5 0.0 copy-done.2
  79.5 0.0 copy-start.7
  79.6 0.6 copy.27
  80.2 0.0 copy-done.7
  80.2 0.0 copy-start.6
  80.2 0.6 copy.28
  80.8 0.1 copy-done.6
  80.9 0.0 copy-start.5
  80.9 0.6 copy.29
  81.4 0.1 copy-done.5
  81.5 0.6 copy.30
  82.1 0.0 copy-done.1
  82.1 0.0 copy-start
  82.1 0.8 copy.31
  82.9 0.5 copy-done
  83.4 0.8 copy.32
Async XLA Ops:
  0.6 0.7 copy-start.3
  76.1 0.7 copy-start.4
  77.3 2.2 %copy-start.2 = (f32[49,192]{1,0:T(8,128)S(1)}, f32[49,192]{1,0:T(8,128)}, u32[]{:S(2)}) copy-start(f32[49,192]{1,0:T(8,128)} %get-tuple-element.33) | copy-start | bytes 112900
  77.3 4.8 %copy-start.1 = (f32[192,768]{1,0:T(8,128)S(1)}, f32[192,768]{1,0:T(8,128)}, u32[]{:S(2)}) copy-start(f32[192,768]{1,0:T(8,128)} %get-tuple-element.37) | copy-start | bytes 1769476
  79.5 0.7 copy-start.7
  80.2 0.7 copy-start.6
  80.9 0.7 copy-start.5
  82.1 1.3 %copy-start = (f32[192,768]{1,0:T(8,128)S(1)}, f32[192,768]{1,0:T(8,128)}, u32[]{:S(2)}) copy-start(f32[192,768]{1,0:T(8,128)} %get-tuple-element.23) | copy-start | bytes 1769476
